TPU v7x, 32 devices: a whole 2x2x4 slice. The times are simulated.
32 devices in a mesh: groups: 2 (over y), replica: 4 (over z), tensor: 4 (over x, core).
Axes of the slice: x: 2, y: 2, z: 4, core: 2. Of those that a mesh axis runs over, the one named last changes fastest.
Arguments:
- queries: bfloat16 [8192, 8192], P(('groups', 'replica'), 'tensor'), parts along dimension 0, may hold values from -160 to 160
- suffix_cache: bfloat16 [8192, 2048], P(('groups', 'replica'), 'tensor'), parts along dimension 0, may hold values from -6 to 6
- cache_pool: bfloat16 [12288, 2048], P(('groups', 'replica'), 'tensor'), parts along dimension 0, may hold values from -6 to 6
- block_table: int32 [8, 4], P(('groups', 'replica')), parts along dimension 0, may hold values from 0 to 5, as said below
- prefix_blocks: int32 [8], P(('groups', 'replica')), parts along dimension 0, may hold values from 1 to 4, as said below
- segment_owner: int32 [128, 1], P(('groups', 'replica')), parts along dimension 0, may hold values from 0 to 3; in each aligned block of 16 rows (0 to 15, 16 to 31, ...) at most 8 rows name the same one
Outputs:
- placed_rows: bfloat16 [16384, 8192], P(('groups', 'replica'), 'tensor'), parts along dimension 0
There are 2 independent parts, one for each index of `groups`. A program takes and returns all parts, laid end to end along the dimension named above; each array names one. Nothing has to cross between parts.
Inputs may be any that keep to these rules, and one draw needn't show every extreme that they name: `block_table`: the 4 entries of a row are distinct. `prefix_blocks`: some request has exactly 4 blocks. `segment_owner`: among the segments of one request at most 8 share an owner, and some owner gets exactly 8.
All inputs are finite; a program needn't handle non-finite values.
Results may differ from a plain program's by a relative error of at most 0.0046.
Values may be sent and summed in bfloat16 or wider, within the bound.
No kernel may reach another device: no remote copies, remote signals or barrier semaphores. Data moves between devices by JAX's collectives and lax.ppermute only.
A program may use at most 192 MiB of HBM per device.

v0:
```python
import functools

import jax
import jax.numpy as jnp
from jax import lax
from jax.experimental import pallas as pl
from jax.experimental.pallas import tpu as pltpu
from jax.sharding import PartitionSpec as P

HEAD_DIM = 128
BLK = 256
MAXB = 4
SEGS = 16
SEG = 64
SCALE = HEAD_DIM ** (-0.5)
LOWEST = -1e38
HEADS_AT_ONCE = 4


def attend_kernel(
    groups, zeros, capacity, me, owner, table, blocks, queries, suffix, pool, *refs
):
    outs, (cache, q_all, o_all, blank, segs, used, todo, place, sems, out_sems, zero_sems) = (
        refs[:-11],
        refs[-11:],
    )
    suffix_rows = suffix.shape[0]
    heads = queries.shape[1] // HEAD_DIM
    group = heads // (suffix.shape[1] // (2 * HEAD_DIM))
    at_once = min(HEADS_AT_ONCE, group)
    rows = at_once * SEG
    prefix = MAXB * BLK

    copies = [pltpu.make_async_copy(suffix, cache.at[pl.ds(prefix, suffix_rows)], sems.at[SEGS])]
    for b in range(MAXB):
        start = pl.multiple_of(table[b] * BLK, BLK)
        to = pl.multiple_of((b + MAXB - blocks[0]) % MAXB * BLK, BLK)
        copies.append(
            pltpu.make_async_copy(
                pool.at[pl.ds(start, BLK)], cache.at[pl.ds(to, BLK)], sems.at[SEGS + 1 + b]
            )
        )
    for copy in copies:
        copy.start()

    @pl.loop(0, segs.shape[0])
    def _(i):
        segs[i] = jnp.int32(-1)

    @pl.loop(0, used.shape[0])
    def _(i):
        used[i] = jnp.int32(0)

    @pl.loop(0, SEGS)
    def _(i):
        distance = owner[i] ^ me[0]
        slot = used[distance]
        used[distance] = slot + 1
        segs[distance * capacity + slot] = i

    def rows_of(ref, seg):
        return ref.at[pl.ds(pl.multiple_of(seg * SEG, SEG), SEG)]

    def fetch(seg):
        return pltpu.make_async_copy(rows_of(queries, seg), rows_of(q_all, seg), sems.at[seg])

    def hand(out, at, seg):
        return pltpu.make_async_copy(rows_of(o_all, seg), rows_of(out, at), out_sems.at[seg])

    def clear(out, at, i):
        return pltpu.make_async_copy(blank, rows_of(out, at), zero_sems.at[i])

    def at_of(distance, slot):
        return (me[0] ^ distance) * capacity + slot

    blank[...] = jnp.zeros_like(blank)
    firsts, found, slots = [], jnp.int32(0), 0
    for out, (distance, first, count, before) in zip(outs, groups):
        firsts.append(slots)

        def look(j, found):
            seg = segs[distance * capacity + first + j]
            at = at_of(distance, first + j) if before is None else before + j

            @pl.when(seg >= 0)
            def _():
                fetch(seg).start()
                todo[found] = seg
                place[found] = slots + j

            @pl.when(seg < 0)
            def _():
                clear(out, at, slots + j).start()

            return jnp.where(seg >= 0, found + 1, found)

        found = lax.fori_loop(0, count, look, found)
        slots += count
    blanks = slots
    for distance, first, count in zeros:
        for j in range(count):
            clear(outs[-1], at_of(distance, first + j), blanks + j).start()
        blanks += count
    for copy in copies:
        copy.wait()

    def attend_rows(seg, count, i):
        first = i * at_once
        low = pl.multiple_of((MAXB - blocks[0]) * BLK, BLK)
        pair = first // group * (2 * HEAD_DIM)

        def column(h):
            return pl.ds(pl.multiple_of((first + h) * HEAD_DIM, HEAD_DIM), HEAD_DIM)

        def cached(offset):
            lanes = pl.ds(pl.multiple_of(pair + offset, HEAD_DIM), HEAD_DIM)
            return cache[pl.ds(low, count * BLK), lanes]

        here = pl.ds(pl.multiple_of(seg * SEG, SEG), SEG)
        q = jnp.concatenate([q_all[here, column(h)] for h in range(at_once)], axis=0)
        s = lax.dot_general(
            q, cached(0), (((1,), (1,)), ((), ())), preferred_element_type=jnp.float32
        )
        parts = [s[:, c : c + HEAD_DIM] for c in range(0, count * BLK, HEAD_DIM)]
        token = lax.broadcasted_iota(jnp.int32, (rows, HEAD_DIM), 0) % SEG + seg * SEG % BLK
        key = lax.broadcasted_iota(jnp.int32, (rows, HEAD_DIM), 1)
        masked = BLK // HEAD_DIM
        for c in range(masked):
            at = len(parts) - masked + c
            parts[at] = jnp.where(key + c * HEAD_DIM <= token, parts[at], LOWEST)
        top = jnp.max(functools.reduce(jnp.maximum, parts), axis=-1, keepdims=True)
        top = jnp.broadcast_to(top, (rows, HEAD_DIM))
        weights = [jnp.exp((part - top) * SCALE) for part in parts]
        total = jnp.sum(functools.reduce(jnp.add, weights), axis=-1, keepdims=True)
        mixed = jnp.dot(
            jnp.concatenate([w.astype(jnp.bfloat16) for w in weights], axis=1),
            cached(HEAD_DIM),
            preferred_element_type=jnp.float32,
        )
        out = (mixed / total).astype(o_all.dtype)
        for h in range(at_once):
            o_all[here, column(h)] = out[h * SEG : (h + 1) * SEG]

    @pl.loop(0, found)
    def _(t):
        seg = todo[t]
        fetch(seg).wait()
        blocks_seen = blocks[0] + seg * SEG // BLK + 1
        for count in range(2, MAXB + suffix_rows // BLK + 1):

            @pl.when(blocks_seen == count)
            def _():
                @pl.loop(0, heads // at_once)
                def _(i):
                    attend_rows(seg, count, i)

        to = place[t]
        for out, first, (distance, slot, count, before) in zip(outs, firsts, groups):
            j = to - first

            @pl.when((j >= 0) & (j < count))
            def _():
                at = at_of(distance, slot + j) if before is None else before + j
                hand(out, at, seg).start()

    @pl.loop(0, found)
    def _(t):
        hand(outs[0], 0, todo[t]).wait()

    first = 0
    for distance, slot, count, _ in groups:

        @pl.loop(0, count)
        def _(j):
            @pl.when(segs[distance * capacity + slot + j] < 0)
            def _():
                clear(outs[0], 0, first + j).wait()

        first += count
    for i in range(slots, blanks):
        clear(outs[0], 0, i).wait()


def attend(groups, whole, capacity, me, owner, table, blocks, queries, suffix, pool):
    replicas = lax.axis_size("replica")
    width = queries.shape[1]
    suffix_rows, columns = suffix.shape
    held = [(k, a, b - a, 0) for k, a, b in groups]
    sizes = [(b - a) * SEG for _, a, b in groups]
    zeros = []
    if whole:
        held.append((0, 0, capacity, None))
        sizes.append(replicas * capacity * SEG)
        zeros = [(k, a, b - a) for k, a, b in whole]
    slots = sum(g[2] for g in held) + sum(z[2] for z in zeros)
    return pl.pallas_call(
        functools.partial(attend_kernel, held, zeros, capacity),
        out_shape=[jax.ShapeDtypeStruct((size, width), queries.dtype) for size in sizes],
        grid_spec=pltpu.PrefetchScalarGridSpec(
            num_scalar_prefetch=4,
            grid=(),
            in_specs=[pl.BlockSpec(memory_space=pl.ANY)] * 3,
            out_specs=[pl.BlockSpec(memory_space=pl.ANY)] * len(sizes),
            scratch_shapes=[
                pltpu.VMEM((suffix_rows + MAXB * BLK, columns), suffix.dtype),
                pltpu.VMEM(queries.shape, queries.dtype),
                pltpu.VMEM(queries.shape, queries.dtype),
                pltpu.VMEM((SEG, width), queries.dtype),
                pltpu.SMEM((replicas * capacity,), jnp.int32),
                pltpu.SMEM((replicas,), jnp.int32),
                pltpu.SMEM((SEGS,), jnp.int32),
                pltpu.SMEM((SEGS,), jnp.int32),
                pltpu.SemaphoreType.DMA((SEGS + MAXB + 1,)),
                pltpu.SemaphoreType.DMA((SEGS,)),
                pltpu.SemaphoreType.DMA((slots,)),
            ],
        ),
        compiler_params=pltpu.CompilerParams(vmem_limit_bytes=56 * 2**20),
        cost_estimate=pl.CostEstimate(flops=2**36, bytes_accessed=SEG * width, transcendentals=0),
    )(me[None], owner, table, blocks, queries, suffix, pool)


def put_kernel(spans, *refs):
    count = len(spans)
    starts, pieces, out, stages = refs[0], refs[1 : 1 + count], refs[2 + count], refs[3 + count :]
    stages, sems = stages[:-1], stages[-1]
    loads = [
        pltpu.make_async_copy(piece, stage, sems.at[0, i])
        for i, (piece, stage) in enumerate(zip(pieces, stages))
    ]
    stores = []
    for i, (span, stage) in enumerate(zip(spans, stages)):
        at = pl.multiple_of(starts[i] * SEG, SEG)
        stores.append(pltpu.make_async_copy(stage, out.at[pl.ds(at, span)], sems.at[1, i]))
    for load in loads:
        load.start()
    for load, store in zip(loads, stores):
        load.wait()
        store.start()
    for store in stores:
        store.wait()


def put(out, pieces):
    rows = [piece for piece, _ in pieces]
    starts = jnp.stack([start for _, start in pieces])
    count = len(rows)
    return pl.pallas_call(
        functools.partial(put_kernel, [r.shape[0] for r in rows]),
        out_shape=jax.ShapeDtypeStruct(out.shape, out.dtype),
        grid_spec=pltpu.PrefetchScalarGridSpec(
            num_scalar_prefetch=1,
            grid=(),
            in_specs=[pl.BlockSpec(memory_space=pl.ANY)] * (count + 1),
            out_specs=pl.BlockSpec(memory_space=pl.ANY),
            scratch_shapes=[pltpu.VMEM(r.shape, r.dtype) for r in rows]
            + [pltpu.SemaphoreType.DMA((2, count))],
        ),
        input_output_aliases={count + 1: 0},
        compiler_params=pltpu.CompilerParams(vmem_limit_bytes=8 * 2**20),
        cost_estimate=pl.CostEstimate(flops=2**27, bytes_accessed=SEG, transcendentals=0),
    )(starts, *rows, out)


def swap(rows, distance):
    size = lax.axis_size("replica")
    return lax.ppermute(rows, "replica", [(i, i ^ distance) for i in range(size)])


def swap_some(out, rows, distance, start, segments):
    def branch(count):
        def run(out, rows):
            if count == 0:
                return out
            return put(out, [(swap(rows[: count * SEG], distance), start)])

        return run

    return lax.switch(segments, [branch(c) for c in range(rows.shape[0] // SEG + 1)], out, rows)


def body(queries, suffix_cache, cache_pool, block_table, prefix_blocks, segment_owner):
    replicas = lax.axis_size("replica")
    me = lax.axis_index("replica").astype(jnp.int32)
    capacity = max(2, 2 * SEGS // replicas)
    base = SEGS // replicas
    owner = segment_owner[:, 0]
    far = list(range(replicas - 1, 0, -1))
    if replicas == 4:
        calls = [[(3, 0, 2)], [(2, 0, 3), (1, 0, 1)], [(2, 3, 4), (3, 2, 4), (1, 1, 4)]]
    else:
        calls = [[(k, 0, base) for k in far]]

    def run(groups, whole=()):
        return attend(
            groups,
            whole,
            capacity,
            me,
            owner,
            block_table[0],
            prefix_blocks,
            queries,
            suffix_cache,
            cache_pool,
        )

    def row_of(k, slot):
        return (me ^ k) * capacity + slot

    theirs = [swap(segment_owner, k) for k in range(1, replicas)]
    sent = []
    for i, call in enumerate(calls):
        made = run(call)
        if sent:
            made, sent[-1] = lax.optimization_barrier((made, sent[-1]))
        owner, made, theirs = lax.optimization_barrier((owner, made, theirs))
        sent.append([(swap(rows, k), row_of(k, a)) for (k, a, _), rows in zip(call, made)])
    over = [(k, base, capacity) for k in far]
    *rest, out = run(over, over)
    distances = jnp.arange(1, replicas, dtype=jnp.int32)
    mine = jnp.sum((owner[None, :] == (me ^ distances)[:, None]).astype(jnp.int32), axis=1)
    given = jnp.sum((jnp.concatenate(theirs, axis=1) == me).astype(jnp.int32), axis=0)
    extra = jnp.clip(jnp.maximum(mine, given) - base, 0, capacity - base)
    early = [piece for part in sent[:-1] for piece in part]
    if early:
        out = put(out, early)
    out = put(out, sent[-1])
    for k, rows in reversed(list(zip(far, rest))):
        out = swap_some(out, rows, k, row_of(k, base), extra[k - 1])
    return out


def solution(mesh):
    in_specs = (
        P(("groups", "replica"), "tensor"),
        P(("groups", "replica"), "tensor"),
        P(("groups", "replica"), "tensor"),
        P(("groups", "replica"), None),
        P(("groups", "replica")),
        P(("groups", "replica"), None),
    )
    out_specs = P(("groups", "replica"), "tensor")
    return jax.shard_map(body, mesh=mesh, in_specs=in_specs, out_specs=out_specs, check_vma=False)
```

profile of v0, /device:TPU:30, one launch (start us, length us, event | category | flops | bytes accessed | tf_op | source)
XLA Modules:
  0.0 143.4 jit_solution(2355740189194799952)
XLA Ops:
  0.0 0.4 collective-permute-start.12
  0.5 1.3 collective-permute-start.14
  1.8 1.7 %collective-permute-start.13 = (s32[16,1]{0,1:T(1,128)}, s32[16,1]{0,1:T(1,128)S(1)}, u32[]{:S(2)}, u32[]{:S(2)}) collective-permute-start(s32[16,1]{0,1:T(1,128)} %param.26), channel_id=1, source_target_pairs={{0,8},{4,12},{8,0},{12,4},{1,9},{5,13},{9,1},{13,5},{2,10},{6,14},... | collective-permute-start | bytes 200 | tf_op jit(solution)/shard_map/ppermute | solution.py:267
  3.5 0.5 add_xor_fusion
  4.7 9.1 %shard_map.69 = bf16[128,2048]{1,0:T(8,128)(2,1)} custom-call(s32[1]{0:T(128)} %bitcast.13.me, s32[16]{0:T(128)} %bitcast.28, s32[4]{0:T(128)} %bitcast.24, s32[1]{0:T(128)S(6)} %copy.55.blocks, bf16[1024,2048]{1,0:T(8,128)(2,1)} %queries.7, bf16[1024,512]{1,0:T(8,128)(2,1)} %suffix.7, bf16[1536,512]{1,0:T(8,128)(2,1)} %pool.7), custom_call_target="tpu_custom_call" | custom-call | flops 68719476736 | bytes 131072 | tf_op jit(solution)/shard_map/pallas_call | solution.py:196
  13.8 0.1 pad_add_fusion.refs_0_
  13.9 0.0 collective-permute-done.12
  13.9 0.0 copy-start.1
  13.9 0.0 collective-permute-done.14
  13.9 0.0 copy-start.3
  13.9 0.0 collective-permute-done.13
  13.9 0.0 copy-start.5
  13.9 2.3 %collective-permute-start.15 = (bf16[128,2048]{1,0:T(8,128)(2,1)}, bf16[128,2048]{1,0:T(8,128)(2,1)S(1)}, u32[]{:S(2)}, u32[]{:S(2)}) collective-permute-start(bf16[128,2048]{1,0:T(8,128)(2,1)} %shard_map.69), channel_id=1, source_target_pairs={{0,12},{4,8},{8,4},{12,0},{1,13},{5,9},{9,5},{13,1},{2,14},{6,10},... | collective-permute-start | bytes 1572872 | tf_op jit(solution)/shard_map/ppermute | solution.py:267
  16.2 16.4 %shard_map.70 = (bf16[192,2048]{1,0:T(8,128)(2,1)}, bf16[64,2048]{1,0:T(8,128)(2,1)}) custom-call(s32[1]{0:T(128)} %bitcast.13.me, s32[16]{0:T(128)} %bitcast.29, s32[4]{0:T(128)} %bitcast.25, s32[1]{0:T(128)S(6)} %copy.55.blocks, bf16[1024,2048]{1,0:T(8,128)(2,1)} %queries.7, bf16[1024,512]{1,0:T(8,128)(2,1)} %suffix.7, bf16[1536,512]{1,0:T(8,128)(2,1)} %pool.7), custom_call_target="tpu_custom_call" | custom-call | flops 68719476736 | bytes 131072 | tf_op jit(solution)/shard_map/pallas_call | solution.py:196
  32.7 0.0 copy-done.1
  32.7 0.0 copy-done.3
  32.7 0.0 copy-done.5
  32.7 0.0 collective-permute-done.15.refs_1_
  32.7 7.9 %collective-permute-start.17 = (bf16[64,2048]{1,0:T(8,128)(2,1)}, bf16[64,2048]{1,0:T(8,128)(2,1)S(1)}, u32[]{:S(2)}, u32[]{:S(2)}) collective-permute-start(bf16[64,2048]{1,0:T(8,128)(2,1)} %get-tuple-element.194), channel_id=1, source_target_pairs={{0,4},{4,0},{8,12},{12,8},{1,5},{5,1},{9,13},{13,9},{2,6},{6,2},{1... | collective-permute-start | bytes 786440 | tf_op jit(solution)/shard_map/ppermute | solution.py:267
  40.6 1.1 collective-permute-start.16
  41.7 18.9 %shard_map.71 = (bf16[64,2048]{1,0:T(8,128)(2,1)}, bf16[128,2048]{1,0:T(8,128)(2,1)}, bf16[192,2048]{1,0:T(8,128)(2,1)}) custom-call(s32[1]{0:T(128)} %bitcast.13.me, s32[16]{0:T(128)} %bitcast.30, s32[4]{0:T(128)} %bitcast.26, s32[1]{0:T(128)S(6)} %copy.55.blocks, bf16[1024,2048]{1,0:T(8,128)(2,1)} %queries.7, bf16[1024,512]{1,0:T(8,128)(2,1)} %suffix.7, ...), custom_call_target="tpu_custom_call" | custom-call | flops 68719476736 | bytes 131072 | tf_op jit(solution)/shard_map/pallas_call | solution.py:196
  60.6 0.0 collective-permute-done.17.refs_3_
  60.6 17.2 %collective-permute-done.16.refs_2_ = bf16[192,2048]{1,0:T(8,128)(2,1)S(1)} collective-permute-done((bf16[192,2048]{1,0:T(8,128)(2,1)}, bf16[192,2048]{1,0:T(8,128)(2,1)S(1)}, u32[]{:S(2)}, u32[]{:S(2)}) %collective-permute-start.16) | collective-permute-done | bytes 786464 | tf_op jit(solution)/shard_map/ppermute | solution.py:267
  77.8 0.0 copy-start.4
  77.8 0.0 copy-start.6
  77.8 0.0 copy-start.8
  77.8 0.1 collective-permute-start.18
  77.9 2.6 %collective-permute-start.19 = (bf16[128,2048]{1,0:T(8,128)(2,1)}, bf16[128,2048]{1,0:T(8,128)(2,1)S(1)}, u32[]{:S(2)}, u32[]{:S(2)}) collective-permute-start(bf16[128,2048]{1,0:T(8,128)(2,1)} %get-tuple-element.206), channel_id=1, source_target_pairs={{0,12},{4,8},{8,4},{12,0},{1,13},{5,9},{9,5},{13,1},{2,14},{6,10},... | collective-permute-start | bytes 1572872 | tf_op jit(solution)/shard_map/ppermute | solution.py:267
  80.5 0.9 collective-permute-start.20
  81.4 28.5 %shard_map.72 = (bf16[256,2048]{1,0:T(8,128)(2,1)S(1)}, bf16[256,2048]{1,0:T(8,128)(2,1)S(1)}, bf16[256,2048]{1,0:T(8,128)(2,1)S(1)}, bf16[2048,2048]{1,0:T(8,128)(2,1)}) custom-call(s32[1]{0:T(128)} %bitcast.13.me, s32[16]{0:T(128)} %bitcast.31, s32[4]{0:T(128)} %bitcast.27, s32[1]{0:T(128)S(6)} %copy.55.blocks, bf16[1024,2048]{1,0:T(8,128)(2,1)} %queries.7, ...), custom_call_target="tpu_custom_call" | custom-call | flops 68719476736 | bytes 131072 | tf_op jit(solution)/shard_map/pallas_call | solution.py:196
  109.9 0.0 copy-done.2
  109.9 0.0 copy-done.4
  109.9 0.0 copy-done.6
  109.9 0.1 convert_reduce_fusion
  110.0 0.0 copy-done.7
  110.0 0.0 copy-done.8
  110.1 0.2 convert_reduce_fusion.1
  110.2 0.6 fusion
  112.7 0.1 pad_add_fusion.1.refs_0_
  112.8 1.8 %shard_map.73.refs_4_ = bf16[2048,2048]{1,0:T(8,128)(2,1)} custom-call(s32[3]{0:T(128)S(1)} %pad_add_fusion.1.refs_0_, bf16[128,2048]{1,0:T(8,128)(2,1)S(1)} %collective-permute-done.15.refs_1_, bf16[192,2048]{1,0:T(8,128)(2,1)S(1)} %collective-permute-done.16.refs_2_, ...), custom_call_target="tpu_custom_call", output_to_operand_aliasing={{}: (4, {})} | custom-call | flops 134217728 | bytes 64 | tf_op jit(solution)/shard_map/pallas_call | solution.py:248
  114.6 0.0 collective-permute-done.18.refs_1_
  114.6 0.0 collective-permute-done.19.refs_2_
  114.7 0.8 collective-permute-done.20.refs_3_
  115.5 1.8 %shard_map.74 = bf16[2048,2048]{1,0:T(8,128)(2,1)} custom-call(s32[3]{0:T(128)S(1)} %pad_add_fusion.refs_0_, bf16[64,2048]{1,0:T(8,128)(2,1)S(1)} %collective-permute-done.18.refs_1_, bf16[128,2048]{1,0:T(8,128)(2,1)S(1)} %collective-permute-done.19.refs_2_, bf16[192,2048]{1,0:T(8,128)(2,1)S(1)} %collective-permute-done.20.refs_3_, ...), custom_call_target="tpu_custom_call", output_to_operand_aliasing={{}: (4, {})} | custom-call | flops 134217728 | bytes 64 | tf_op jit(solution)/shard_map/pallas_call | solution.py:248
  117.4 25.8 %conditional.5 = (bf16[2048,2048]{1,0:T(8,128)(2,1)}) conditional(s32[]{:T(128)} %bitcast.15, bf16[2048,2048]{1,0:T(8,128)(2,1)} %get-tuple-element.244, (s32[]{:T(128)}, bf16[256,2048]{1,0:T(8,128)(2,1)S(1)}, bf16[2048,2048]{1,0:T(8,128)(2,1)}) %tuple.62, (s32[]{:T(128)}, bf16[256,2048]{1,0:T(8,128)(2,1)S(1)}, ...), branch_computations={%region_12.13_spmd, %region_13.14_spmd, %region_14.15_spmd, %regio... | conditional | flops 134217728 | bytes 4718716 | solution.py:279
  117.5 1.5 %collective-permute-start.11 = (bf16[256,2048]{1,0:T(8,128)(2,1)S(1)}, bf16[256,2048]{1,0:T(8,128)(2,1)S(1)}, u32[]{:S(2)}, u32[]{:S(2)}) collective-permute-start(bf16[256,2048]{1,0:T(8,128)(2,1)S(1)} %get-tuple-element.140), channel_id=1, source_target_pairs={{0,12},{4,8},{8,4},{12,0},{1,13},{5,9},{9,5},{13,1},{2,14},{6,10},... | collective-permute-start | bytes 3145736 | tf_op jit(solution)/shard_map/cond/branch_4_fun/ppermute | solution.py:267
  119.0 23.2 %collective-permute-done.11.refs_1_ = bf16[256,2048]{1,0:T(8,128)(2,1)S(1)} collective-permute-done((bf16[256,2048]{1,0:T(8,128)(2,1)S(1)}, bf16[256,2048]{1,0:T(8,128)(2,1)S(1)}, u32[]{:S(2)}, u32[]{:S(2)}) %collective-permute-start.11) | collective-permute-done | bytes 1048608 | tf_op jit(solution)/shard_map/cond/branch_4_fun/ppermute | solution.py:267
  142.2 1.1 branch_4_fun.5
  (5 shorter events, 0.1 us)
Async XLA Ops:
  0.0 13.9 %collective-permute-start.12 = (s32[16,1]{0,1:T(1,128)}, s32[16,1]{0,1:T(1,128)S(1)}, u32[]{:S(2)}, u32[]{:S(2)}) collective-permute-start(s32[16,1]{0,1:T(1,128)} %param.26), channel_id=1, source_target_pairs={{0,4},{4,0},{8,12},{12,8},{1,5},{5,1},{9,13},{13,9},{2,6},{6,2},{1... | collective-permute-start | bytes 200 | tf_op jit(solution)/shard_map/ppermute | solution.py:267
  0.5 13.4 %collective-permute-start.14 = (s32[16,1]{0,1:T(1,128)}, s32[16,1]{0,1:T(1,128)S(1)}, u32[]{:S(2)}, u32[]{:S(2)}) collective-permute-start(s32[16,1]{0,1:T(1,128)} %param.26), channel_id=1, source_target_pairs={{0,12},{4,8},{8,4},{12,0},{1,13},{5,9},{9,5},{13,1},{2,14},{6,10},... | collective-permute-start | bytes 200 | tf_op jit(solution)/shard_map/ppermute | solution.py:267
  1.8 12.1 %collective-permute-start.13 = (s32[16,1]{0,1:T(1,128)}, s32[16,1]{0,1:T(1,128)S(1)}, u32[]{:S(2)}, u32[]{:S(2)}) collective-permute-start(s32[16,1]{0,1:T(1,128)} %param.26), channel_id=1, source_target_pairs={{0,8},{4,12},{8,0},{12,4},{1,9},{5,13},{9,1},{13,5},{2,10},{6,14},... | collective-permute-start | bytes 200 | tf_op jit(solution)/shard_map/ppermute | solution.py:267
  13.9 18.8 %copy-start.1 = (s32[16,1]{0,1:T(1,128)}, s32[16,1]{0,1:T(1,128)S(1)}, u32[]{:S(2)}) copy-start(s32[16,1]{0,1:T(1,128)S(1)} %collective-permute-done.12) | copy-start | bytes 196
  13.9 18.8 %copy-start.3 = (s32[16,1]{0,1:T(1,128)}, s32[16,1]{0,1:T(1,128)S(1)}, u32[]{:S(2)}) copy-start(s32[16,1]{0,1:T(1,128)S(1)} %collective-permute-done.14) | copy-start | bytes 196
  13.9 18.8 %copy-start.5 = (s32[16,1]{0,1:T(1,128)}, s32[16,1]{0,1:T(1,128)S(1)}, u32[]{:S(2)}) copy-start(s32[16,1]{0,1:T(1,128)S(1)} %collective-permute-done.13) | copy-start | bytes 196
  13.9 18.8 %collective-permute-start.15 = (bf16[128,2048]{1,0:T(8,128)(2,1)}, bf16[128,2048]{1,0:T(8,128)(2,1)S(1)}, u32[]{:S(2)}, u32[]{:S(2)}) collective-permute-start(bf16[128,2048]{1,0:T(8,128)(2,1)} %shard_map.69), channel_id=1, source_target_pairs={{0,12},{4,8},{8,4},{12,0},{1,13},{5,9},{9,5},{13,1},{2,14},{6,10},... | collective-permute-start | bytes 1572872 | tf_op jit(solution)/shard_map/ppermute | solution.py:267
  32.7 27.9 %collective-permute-start.17 = (bf16[64,2048]{1,0:T(8,128)(2,1)}, bf16[64,2048]{1,0:T(8,128)(2,1)S(1)}, u32[]{:S(2)}, u32[]{:S(2)}) collective-permute-start(bf16[64,2048]{1,0:T(8,128)(2,1)} %get-tuple-element.194), channel_id=1, source_target_pairs={{0,4},{4,0},{8,12},{12,8},{1,5},{5,1},{9,13},{13,9},{2,6},{6,2},{1... | collective-permute-start | bytes 786440 | tf_op jit(solution)/shard_map/ppermute | solution.py:267
  40.6 37.2 %collective-permute-start.16 = (bf16[192,2048]{1,0:T(8,128)(2,1)}, bf16[192,2048]{1,0:T(8,128)(2,1)S(1)}, u32[]{:S(2)}, u32[]{:S(2)}) collective-permute-start(bf16[192,2048]{1,0:T(8,128)(2,1)} %get-tuple-element.193), channel_id=1, source_target_pairs={{0,8},{4,12},{8,0},{12,4},{1,9},{5,13},{9,1},{13,5},{2,10},{6,14},... | collective-permute-start | bytes 2359304 | tf_op jit(solution)/shard_map/ppermute | solution.py:267
  77.8 32.1 %copy-start.2 = (s32[16,1]{0,1:T(1,128)S(1)}, s32[16,1]{0,1:T(1,128)}, u32[]{:S(2)}) copy-start(s32[16,1]{0,1:T(1,128)} %copy-done.1) | copy-start | bytes 196
  77.8 32.1 %copy-start.4 = (s32[16,1]{0,1:T(1,128)S(1)}, s32[16,1]{0,1:T(1,128)}, u32[]{:S(2)}) copy-start(s32[16,1]{0,1:T(1,128)} %copy-done.3) | copy-start | bytes 196
  77.8 32.1 %copy-start.6 = (s32[16,1]{0,1:T(1,128)S(1)}, s32[16,1]{0,1:T(1,128)}, u32[]{:S(2)}) copy-start(s32[16,1]{0,1:T(1,128)} %copy-done.5) | copy-start | bytes 196
  77.8 32.2 %copy-start.7 = (s32[16,1]{0,1:T(1,128)S(1)}, s32[16,1]{0,1:T(1,128)}, u32[]{:S(2)}) copy-start(s32[16,1]{0,1:T(1,128)} %param.26) | copy-start | bytes 196
  77.8 32.2 %copy-start.8 = (s32[3]{0:T(128)S(1)}, s32[3]{0:T(128)}, u32[]{:S(2)}) copy-start(s32[3]{0:T(128)} %add_xor_fusion) | copy-start | bytes 40
  77.8 36.8 %collective-permute-start.18 = (bf16[64,2048]{1,0:T(8,128)(2,1)}, bf16[64,2048]{1,0:T(8,128)(2,1)S(1)}, u32[]{:S(2)}, u32[]{:S(2)}) collective-permute-start(bf16[64,2048]{1,0:T(8,128)(2,1)} %get-tuple-element.205), channel_id=1, source_target_pairs={{0,8},{4,12},{8,0},{12,4},{1,9},{5,13},{9,1},{13,5},{2,10},{6,14},... | collective-permute-start | bytes 786440 | tf_op jit(solution)/shard_map/ppermute | solution.py:267
  77.9 36.7 %collective-permute-start.19 = (bf16[128,2048]{1,0:T(8,128)(2,1)}, bf16[128,2048]{1,0:T(8,128)(2,1)S(1)}, u32[]{:S(2)}, u32[]{:S(2)}) collective-permute-start(bf16[128,2048]{1,0:T(8,128)(2,1)} %get-tuple-element.206), channel_id=1, source_target_pairs={{0,12},{4,8},{8,4},{12,0},{1,13},{5,9},{9,5},{13,1},{2,14},{6,10},... | collective-permute-start | bytes 1572872 | tf_op jit(solution)/shard_map/ppermute | solution.py:267
  80.5 35.0 %collective-permute-start.20 = (bf16[192,2048]{1,0:T(8,128)(2,1)}, bf16[192,2048]{1,0:T(8,128)(2,1)S(1)}, u32[]{:S(2)}, u32[]{:S(2)}) collective-permute-start(bf16[192,2048]{1,0:T(8,128)(2,1)} %get-tuple-element.207), channel_id=1, source_target_pairs={{0,4},{4,0},{8,12},{12,8},{1,5},{5,1},{9,13},{13,9},{2,6},{6,2},{1... | collective-permute-start | bytes 2359304 | tf_op jit(solution)/shard_map/ppermute | solution.py:267
  117.5 24.7 %collective-permute-start.11 = (bf16[256,2048]{1,0:T(8,128)(2,1)S(1)}, bf16[256,2048]{1,0:T(8,128)(2,1)S(1)}, u32[]{:S(2)}, u32[]{:S(2)}) collective-permute-start(bf16[256,2048]{1,0:T(8,128)(2,1)S(1)} %get-tuple-element.140), channel_id=1, source_target_pairs={{0,12},{4,8},{8,4},{12,0},{1,13},{5,9},{9,5},{13,1},{2,14},{6,10},... | collective-permute-start | bytes 3145736 | tf_op jit(solution)/shard_map/cond/branch_4_fun/ppermute | solution.py:267
where the time goes:
time: 142 us; the launch traced here: 143 us
  Pallas kernels  77.7 us (55%)
  waiting for transfers between devices  41.3 us (29%)
  starting transfers between devices  19.8 us (14%)
  between operations  2.84 us (2%)
    pallas_call x4, Pallas kernels, attend(): pl.pallas_call(functools.partial(attend_kernel, held, zeros, capacity), o...  73 us
    ppermute x10, waiting for transfers between devices, swap(): lax.ppermute(rows, 'replica', [(i, i ^ distance) for i in range(size)])  41.3 us
    ppermute x10, starting transfers between devices, swap(): lax.ppermute(rows, 'replica', [(i, i ^ distance) for i in range(size)])  19.8 us
    pallas_call x3, Pallas kernels, put(): pl.pallas_call(functools.partial(put_kernel, [r.shape[0] for r in rows]),...  4.74 us
  transfers between devices with their start and end apart: 10, of which 3 were waited for; matrix products, arithmetic and copies ran while one was open for 1% of the time, Pallas kernels for 52%

commit v1 on v0

--- a/solution.py
+++ b/solution.py
@@ -18,10 +18,10 @@
 
 
 def attend_kernel(
-    groups, zeros, capacity, me, owner, table, blocks, queries, suffix, pool, *refs
+    groups, zeros, fill, capacity, skip, me, owner, table, blocks, queries, suffix, pool, *refs
 ):
     outs, (cache, q_all, o_all, blank, segs, used, todo, place, sems, out_sems, zero_sems) = (
-        refs[:-11],
+        refs[skip:-11],
         refs[-11:],
     )
     suffix_rows = suffix.shape[0]
@@ -94,7 +94,22 @@
 
             return jnp.where(seg >= 0, found + 1, found)
 
-        found = lax.fori_loop(0, count, look, found)
+        if before is None:
+            earlier, sends, quota = fill
+
+            def room(parts, limit, taken):
+                busy = sum((jnp.clip(used[k] - a, 0, b - a) for k, a, b in parts), jnp.int32(0))
+                return taken + jnp.clip(limit - busy, 0, used[0] - taken)
+
+            low = jnp.int32(0)
+            for parts, limit in earlier:
+                low = room(parts, limit, low)
+            high = used[0] if quota is None else room(sends, quota, low)
+            found = lax.fori_loop(low, high, look, found)
+            if quota is None:
+                found = lax.fori_loop(used[0], capacity, look, found)
+        else:
+            found = lax.fori_loop(0, count, look, found)
         slots += count
     blanks = slots
     for distance, first, count in zeros:
@@ -168,9 +183,10 @@
         hand(outs[0], 0, todo[t]).wait()
 
     first = 0
-    for distance, slot, count, _ in groups:
-
-        @pl.loop(0, count)
+    for distance, slot, count, before in groups:
+        whole = before is None and fill[2] is not None
+
+        @pl.loop(0, 0 if whole else count)
         def _(j):
             @pl.when(segs[distance * capacity + slot + j] < 0)
             def _():
@@ -181,25 +197,25 @@
         clear(outs[0], 0, i).wait()
 
 
-def attend(groups, whole, capacity, me, owner, table, blocks, queries, suffix, pool):
+def attend(groups, fill, zeros, old, capacity, me, owner, table, blocks, queries, suffix, pool):
     replicas = lax.axis_size("replica")
     width = queries.shape[1]
     suffix_rows, columns = suffix.shape
     held = [(k, a, b - a, 0) for k, a, b in groups]
     sizes = [(b - a) * SEG for _, a, b in groups]
-    zeros = []
-    if whole:
+    if fill:
         held.append((0, 0, capacity, None))
         sizes.append(replicas * capacity * SEG)
-        zeros = [(k, a, b - a) for k, a, b in whole]
+    zeros = [(k, a, b - a) for k, a, b in zeros]
     slots = sum(g[2] for g in held) + sum(z[2] for z in zeros)
+    inputs = [queries, suffix, pool] + ([] if old is None else [old])
     return pl.pallas_call(
-        functools.partial(attend_kernel, held, zeros, capacity),
+        functools.partial(attend_kernel, held, zeros, fill, capacity, len(inputs) - 3),
         out_shape=[jax.ShapeDtypeStruct((size, width), queries.dtype) for size in sizes],
         grid_spec=pltpu.PrefetchScalarGridSpec(
             num_scalar_prefetch=4,
             grid=(),
-            in_specs=[pl.BlockSpec(memory_space=pl.ANY)] * 3,
+            in_specs=[pl.BlockSpec(memory_space=pl.ANY)] * len(inputs),
             out_specs=[pl.BlockSpec(memory_space=pl.ANY)] * len(sizes),
             scratch_shapes=[
                 pltpu.VMEM((suffix_rows + MAXB * BLK, columns), suffix.dtype),
@@ -215,9 +231,10 @@
                 pltpu.SemaphoreType.DMA((slots,)),
             ],
         ),
+        input_output_aliases={} if old is None else {7: len(sizes) - 1},
         compiler_params=pltpu.CompilerParams(vmem_limit_bytes=56 * 2**20),
         cost_estimate=pl.CostEstimate(flops=2**36, bytes_accessed=SEG * width, transcendentals=0),
-    )(me[None], owner, table, blocks, queries, suffix, pool)
+    )(me[None], owner, table, blocks, *inputs)
 
 
 def put_kernel(spans, *refs):
@@ -291,10 +308,14 @@
     else:
         calls = [[(k, 0, base) for k in far]]
 
-    def run(groups, whole=()):
+    over = [(k, base, capacity) for k in far]
+
+    def run(groups, fill=None, zeros=(), old=None):
         return attend(
             groups,
-            whole,
+            fill,
+            zeros,
+            old,
             capacity,
             me,
             owner,
@@ -309,15 +330,20 @@
         return (me ^ k) * capacity + slot
 
     theirs = [swap(segment_owner, k) for k in range(1, replicas)]
-    sent = []
+    sent, out, quotas = [], None, []
     for i, call in enumerate(calls):
-        made = run(call)
+        if i == 0:
+            made = run(call)
+        else:
+            quota = sum(b - a for _, a, b in call)
+            zeros = over if out is None else ()
+            *made, out = run(call, (list(quotas), call, quota), zeros, out)
+            quotas.append((call, quota))
         if sent:
             made, sent[-1] = lax.optimization_barrier((made, sent[-1]))
         owner, made, theirs = lax.optimization_barrier((owner, made, theirs))
         sent.append([(swap(rows, k), row_of(k, a)) for (k, a, _), rows in zip(call, made)])
-    over = [(k, base, capacity) for k in far]
-    *rest, out = run(over, over)
+    *rest, out = run(over, (quotas, over, None), over if out is None else (), out)
     distances = jnp.arange(1, replicas, dtype=jnp.int32)
     mine = jnp.sum((owner[None, :] == (me ^ distances)[:, None]).astype(jnp.int32), axis=1)
     given = jnp.sum((jnp.concatenate(theirs, axis=1) == me).astype(jnp.int32), axis=0)

time: 142 us -> 149 us (1.049)
  the two profiles are of different devices: /device:TPU:30 before, /device:TPU:0 now
where the time goes in v1:
time: 149 us
  Pallas kernels  63.9 us (43%)
  waiting for transfers between devices  46.6 us (31%)
  starting transfers between devices  34.3 us (23%)
  between operations  2.76 us (2%)
    pallas_call x4, Pallas kernels, attend(): pl.pallas_call(functools.partial(attend_kernel, held, zeros, fill, capaci...  59.1 us
    ppermute x10, waiting for transfers between devices, swap(): lax.ppermute(rows, 'replica', [(i, i ^ distance) for i in range(size)])  46.6 us
    ppermute x10, starting transfers between devices, swap(): lax.ppermute(rows, 'replica', [(i, i ^ distance) for i in range(size)])  34.3 us
    pallas_call x3, Pallas kernels, put(): pl.pallas_call(functools.partial(put_kernel, [r.shape[0] for r in rows]),...  4.74 us
  transfers between devices with their start and end apart: 10, of which 3 were waited for; matrix products, arithmetic and copies ran while one was open for 1% of the time, Pallas kernels for 41%

profile of v1, /device:TPU:0, one launch (start us, length us, event | category | flops | bytes accessed | tf_op | source)
XLA Modules:
  0.0 149.3 jit_solution(13100503435809325567)
XLA Ops:
  0.0 3.0 %collective-permute-start.12 = (s32[16,1]{0,1:T(1,128)}, s32[16,1]{0,1:T(1,128)S(1)}, u32[]{:S(2)}, u32[]{:S(2)}) collective-permute-start(s32[16,1]{0,1:T(1,128)} %param.26), channel_id=1, source_target_pairs={{0,4},{4,0},{8,12},{12,8},{1,5},{5,1},{9,13},{13,9},{2,6},{6,2},{1... | collective-permute-start | bytes 200 | tf_op jit(solution)/shard_map/ppermute | solution.py:284
  3.0 2.6 %collective-permute-start.13 = (s32[16,1]{0,1:T(1,128)}, s32[16,1]{0,1:T(1,128)S(1)}, u32[]{:S(2)}, u32[]{:S(2)}) collective-permute-start(s32[16,1]{0,1:T(1,128)} %param.26), channel_id=1, source_target_pairs={{0,8},{4,12},{8,0},{12,4},{1,9},{5,13},{9,1},{13,5},{2,10},{6,14},... | collective-permute-start | bytes 200 | tf_op jit(solution)/shard_map/ppermute | solution.py:284
  5.6 0.0 collective-permute-start.14
  6.3 0.5 add_xor_fusion
  6.8 8.9 %shard_map.69 = bf16[128,2048]{1,0:T(8,128)(2,1)} custom-call(s32[1]{0:T(128)} %bitcast.13.me, s32[16]{0:T(128)} %bitcast.28, s32[4]{0:T(128)} %bitcast.24, s32[1]{0:T(128)S(6)} %copy.59.blocks, bf16[1024,2048]{1,0:T(8,128)(2,1)} %queries.7, bf16[1024,512]{1,0:T(8,128)(2,1)} %suffix.7, bf16[1536,512]{1,0:T(8,128)(2,1)} %pool.7), custom_call_target="tpu_custom_call" | custom-call | flops 68719476736 | bytes 131072 | tf_op jit(solution)/shard_map/pallas_call | solution.py:212
  15.7 0.1 pad_add_fusion.refs_0_
  15.7 0.0 collective-permute-done.12
  15.8 0.0 copy-start.1
  15.8 0.0 collective-permute-done.13
  15.8 0.0 copy-start.3
  15.8 0.0 collective-permute-done.14
  15.8 0.0 copy-start.5
  15.8 3.9 %collective-permute-start.15 = (bf16[128,2048]{1,0:T(8,128)(2,1)}, bf16[128,2048]{1,0:T(8,128)(2,1)S(1)}, u32[]{:S(2)}, u32[]{:S(2)}) collective-permute-start(bf16[128,2048]{1,0:T(8,128)(2,1)} %shard_map.69), channel_id=1, source_target_pairs={{0,12},{4,8},{8,4},{12,0},{1,13},{5,9},{9,5},{13,1},{2,14},{6,10},... | collective-permute-start | bytes 1572872 | tf_op jit(solution)/shard_map/ppermute | solution.py:284
  19.7 12.6 %shard_map.70 = (bf16[192,2048]{1,0:T(8,128)(2,1)}, bf16[64,2048]{1,0:T(8,128)(2,1)}, bf16[2048,2048]{1,0:T(8,128)(2,1)}) custom-call(s32[1]{0:T(128)} %bitcast.13.me, s32[16]{0:T(128)} %bitcast.29, s32[4]{0:T(128)} %bitcast.25, s32[1]{0:T(128)S(6)} %copy.59.blocks, bf16[1024,2048]{1,0:T(8,128)(2,1)} %queries.7, bf16[1024,512]{1,0:T(8,128)(2,1)} %suffix.7, ...), custom_call_target="tpu_custom_call" | custom-call | flops 68719476736 | bytes 131072 | tf_op jit(solution)/shard_map/pallas_call | solution.py:212
  32.3 0.0 copy-done.1
  32.3 0.0 copy-done.3
  32.3 0.0 copy-done.5
  32.3 0.0 collective-permute-done.15.refs_1_
  32.3 11.0 %collective-permute-start.16 = (bf16[192,2048]{1,0:T(8,128)(2,1)}, bf16[192,2048]{1,0:T(8,128)(2,1)S(1)}, u32[]{:S(2)}, u32[]{:S(2)}) collective-permute-start(bf16[192,2048]{1,0:T(8,128)(2,1)} %get-tuple-element.196), channel_id=1, source_target_pairs={{0,8},{4,12},{8,0},{12,4},{1,9},{5,13},{9,1},{13,5},{2,10},{6,14},... | collective-permute-start | bytes 2359304 | tf_op jit(solution)/shard_map/ppermute | solution.py:284
  43.3 0.0 collective-permute-start.17
  43.3 22.2 %shard_map.71 = (bf16[64,2048]{1,0:T(8,128)(2,1)}, bf16[128,2048]{1,0:T(8,128)(2,1)}, bf16[192,2048]{1,0:T(8,128)(2,1)}, bf16[2048,2048]{1,0:T(8,128)(2,1)}) custom-call(s32[1]{0:T(128)} %bitcast.13.me, s32[16]{0:T(128)} %bitcast.30, s32[4]{0:T(128)} %bitcast.26, s32[1]{0:T(128)S(6)} %copy.59.blocks, ...), custom_call_target="tpu_custom_call", output_to_operand_aliasing={{3}: (7, {})} | custom-call | flops 68719476736 | bytes 131072 | tf_op jit(solution)/shard_map/pallas_call | solution.py:212
  65.5 0.0 collective-permute-done.17.refs_3_
  65.6 11.1 %collective-permute-done.16.refs_2_ = bf16[192,2048]{1,0:T(8,128)(2,1)S(1)} collective-permute-done((bf16[192,2048]{1,0:T(8,128)(2,1)}, bf16[192,2048]{1,0:T(8,128)(2,1)S(1)}, u32[]{:S(2)}, u32[]{:S(2)}) %collective-permute-start.16) | collective-permute-done | bytes 786464 | tf_op jit(solution)/shard_map/ppermute | solution.py:284
  76.6 0.6 collective-permute-start.20
  77.2 2.7 %collective-permute-start.19 = (bf16[128,2048]{1,0:T(8,128)(2,1)}, bf16[128,2048]{1,0:T(8,128)(2,1)S(1)}, u32[]{:S(2)}, u32[]{:S(2)}) collective-permute-start(bf16[128,2048]{1,0:T(8,128)(2,1)} %get-tuple-element.209), channel_id=1, source_target_pairs={{0,12},{4,8},{8,4},{12,0},{1,13},{5,9},{9,5},{13,1},{2,14},{6,10},... | collective-permute-start | bytes 1572872 | tf_op jit(solution)/shard_map/ppermute | solution.py:284
  79.9 0.6 collective-permute-start.18
  80.5 0.0 copy-start.2
  80.5 0.0 copy-start.4
  80.5 0.0 copy-start.8
  80.5 15.4 %shard_map.72 = (bf16[256,2048]{1,0:T(8,128)(2,1)S(1)}, bf16[256,2048]{1,0:T(8,128)(2,1)S(1)}, bf16[256,2048]{1,0:T(8,128)(2,1)S(1)}, bf16[2048,2048]{1,0:T(8,128)(2,1)}) custom-call(s32[1]{0:T(128)} %bitcast.13.me, s32[16]{0:T(128)} %bitcast.31, s32[4]{0:T(128)} %bitcast.27, s32[1]{0:T(128)S(6)} %copy.59.blocks, ...), custom_call_target="tpu_custom_call", output_to_operand_aliasing={{3}: (7, {})} | custom-call | flops 68719476736 | bytes 131072 | tf_op jit(solution)/shard_map/pallas_call | solution.py:212
  96.0 0.0 copy-done.2
  96.0 0.0 copy-done.4
  96.0 0.0 copy-done.6
  96.0 0.1 convert_reduce_fusion
  96.1 0.0 copy-done.7
  96.1 0.0 copy-done.8
  96.1 0.2 convert_reduce_fusion.1
  96.3 0.6 fusion
  98.7 0.1 pad_add_fusion.1.refs_0_
  98.8 1.8 %shard_map.73.refs_4_ = bf16[2048,2048]{1,0:T(8,128)(2,1)} custom-call(s32[3]{0:T(128)S(1)} %pad_add_fusion.1.refs_0_, bf16[128,2048]{1,0:T(8,128)(2,1)S(1)} %collective-permute-done.15.refs_1_, bf16[192,2048]{1,0:T(8,128)(2,1)S(1)} %collective-permute-done.16.refs_2_, ...), custom_call_target="tpu_custom_call", output_to_operand_aliasing={{}: (4, {})} | custom-call | flops 134217728 | bytes 64 | tf_op jit(solution)/shard_map/pallas_call | solution.py:265
  100.6 14.2 %collective-permute-done.18.refs_1_ = bf16[64,2048]{1,0:T(8,128)(2,1)S(1)} collective-permute-done((bf16[64,2048]{1,0:T(8,128)(2,1)}, bf16[64,2048]{1,0:T(8,128)(2,1)S(1)}, u32[]{:S(2)}, u32[]{:S(2)}) %collective-permute-start.18) | collective-permute-done | bytes 262176 | tf_op jit(solution)/shard_map/ppermute | solution.py:284
  114.8 0.0 collective-permute-done.19.refs_2_
  114.8 0.0 collective-permute-done.20.refs_3_
  114.8 1.8 %shard_map.74 = bf16[2048,2048]{1,0:T(8,128)(2,1)} custom-call(s32[3]{0:T(128)S(1)} %pad_add_fusion.refs_0_, bf16[64,2048]{1,0:T(8,128)(2,1)S(1)} %collective-permute-done.18.refs_1_, bf16[128,2048]{1,0:T(8,128)(2,1)S(1)} %collective-permute-done.19.refs_2_, bf16[192,2048]{1,0:T(8,128)(2,1)S(1)} %collective-permute-done.20.refs_3_, ...), custom_call_target="tpu_custom_call", output_to_operand_aliasing={{}: (4, {})} | custom-call | flops 134217728 | bytes 64 | tf_op jit(solution)/shard_map/pallas_call | solution.py:265
  116.7 32.4 %conditional.4 = (bf16[2048,2048]{1,0:T(8,128)(2,1)}) conditional(s32[]{:T(128)} %bitcast.16, bf16[2048,2048]{1,0:T(8,128)(2,1)} %get-tuple-element.247, (s32[]{:T(128)}, bf16[256,2048]{1,0:T(8,128)(2,1)S(1)}, bf16[2048,2048]{1,0:T(8,128)(2,1)}, s32[]{:T(128)}) %tuple.61, (s32[]{:T(128)}, ...), branch_computations={%region_7.8_spmd, %region_8.9_spmd, %region_9.10_spmd, %region_10.... | conditional | flops 134217728 | bytes 4718716 | solution.py:296
  116.8 10.0 %collective-permute-start.7 = (bf16[256,2048]{1,0:T(8,128)(2,1)S(1)}, bf16[256,2048]{1,0:T(8,128)(2,1)S(1)}, u32[]{:S(2)}, u32[]{:S(2)}) collective-permute-start(bf16[256,2048]{1,0:T(8,128)(2,1)S(1)} %get-tuple-element.128), channel_id=1, source_target_pairs={{0,8},{4,12},{8,0},{12,4},{1,9},{5,13},{9,1},{13,5},{2,10},{6,14},... | collective-permute-start | bytes 3145736 | tf_op jit(solution)/shard_map/cond/branch_4_fun/ppermute | solution.py:284
  126.8 21.3 %collective-permute-done.7.refs_1_ = bf16[256,2048]{1,0:T(8,128)(2,1)S(1)} collective-permute-done((bf16[256,2048]{1,0:T(8,128)(2,1)S(1)}, bf16[256,2048]{1,0:T(8,128)(2,1)S(1)}, u32[]{:S(2)}, u32[]{:S(2)}) %collective-permute-start.7) | collective-permute-done | bytes 1048608 | tf_op jit(solution)/shard_map/cond/branch_4_fun/ppermute | solution.py:284
  148.0 1.1 branch_4_fun.4
  (5 shorter events, 0.1 us)
Async XLA Ops:
  0.0 15.8 %collective-permute-start.12 = (s32[16,1]{0,1:T(1,128)}, s32[16,1]{0,1:T(1,128)S(1)}, u32[]{:S(2)}, u32[]{:S(2)}) collective-permute-start(s32[16,1]{0,1:T(1,128)} %param.26), channel_id=1, source_target_pairs={{0,4},{4,0},{8,12},{12,8},{1,5},{5,1},{9,13},{13,9},{2,6},{6,2},{1... | collective-permute-start | bytes 200 | tf_op jit(solution)/shard_map/ppermute | solution.py:284
  3.0 12.7 %collective-permute-start.13 = (s32[16,1]{0,1:T(1,128)}, s32[16,1]{0,1:T(1,128)S(1)}, u32[]{:S(2)}, u32[]{:S(2)}) collective-permute-start(s32[16,1]{0,1:T(1,128)} %param.26), channel_id=1, source_target_pairs={{0,8},{4,12},{8,0},{12,4},{1,9},{5,13},{9,1},{13,5},{2,10},{6,14},... | collective-permute-start | bytes 200 | tf_op jit(solution)/shard_map/ppermute | solution.py:284
  5.6 10.2 %collective-permute-start.14 = (s32[16,1]{0,1:T(1,128)}, s32[16,1]{0,1:T(1,128)S(1)}, u32[]{:S(2)}, u32[]{:S(2)}) collective-permute-start(s32[16,1]{0,1:T(1,128)} %param.26), channel_id=1, source_target_pairs={{0,12},{4,8},{8,4},{12,0},{1,13},{5,9},{9,5},{13,1},{2,14},{6,10},... | collective-permute-start | bytes 200 | tf_op jit(solution)/shard_map/ppermute | solution.py:284
  15.8 16.5 %copy-start.1 = (s32[16,1]{0,1:T(1,128)}, s32[16,1]{0,1:T(1,128)S(1)}, u32[]{:S(2)}) copy-start(s32[16,1]{0,1:T(1,128)S(1)} %collective-permute-done.12) | copy-start | bytes 196
  15.8 16.5 %copy-start.3 = (s32[16,1]{0,1:T(1,128)}, s32[16,1]{0,1:T(1,128)S(1)}, u32[]{:S(2)}) copy-start(s32[16,1]{0,1:T(1,128)S(1)} %collective-permute-done.13) | copy-start | bytes 196
  15.8 16.5 %copy-start.5 = (s32[16,1]{0,1:T(1,128)}, s32[16,1]{0,1:T(1,128)S(1)}, u32[]{:S(2)}) copy-start(s32[16,1]{0,1:T(1,128)S(1)} %collective-permute-done.14) | copy-start | bytes 196
  15.8 16.5 %collective-permute-start.15 = (bf16[128,2048]{1,0:T(8,128)(2,1)}, bf16[128,2048]{1,0:T(8,128)(2,1)S(1)}, u32[]{:S(2)}, u32[]{:S(2)}) collective-permute-start(bf16[128,2048]{1,0:T(8,128)(2,1)} %shard_map.69), channel_id=1, source_target_pairs={{0,12},{4,8},{8,4},{12,0},{1,13},{5,9},{9,5},{13,1},{2,14},{6,10},... | collective-permute-start | bytes 1572872 | tf_op jit(solution)/shard_map/ppermute | solution.py:284
  32.3 44.3 %collective-permute-start.16 = (bf16[192,2048]{1,0:T(8,128)(2,1)}, bf16[192,2048]{1,0:T(8,128)(2,1)S(1)}, u32[]{:S(2)}, u32[]{:S(2)}) collective-permute-start(bf16[192,2048]{1,0:T(8,128)(2,1)} %get-tuple-element.196), channel_id=1, source_target_pairs={{0,8},{4,12},{8,0},{12,4},{1,9},{5,13},{9,1},{13,5},{2,10},{6,14},... | collective-permute-start | bytes 2359304 | tf_op jit(solution)/shard_map/ppermute | solution.py:284
  43.3 22.3 %collective-permute-start.17 = (bf16[64,2048]{1,0:T(8,128)(2,1)}, bf16[64,2048]{1,0:T(8,128)(2,1)S(1)}, u32[]{:S(2)}, u32[]{:S(2)}) collective-permute-start(bf16[64,2048]{1,0:T(8,128)(2,1)} %get-tuple-element.197), channel_id=1, source_target_pairs={{0,4},{4,0},{8,12},{12,8},{1,5},{5,1},{9,13},{13,9},{2,6},{6,2},{1... | collective-permute-start | bytes 786440 | tf_op jit(solution)/shard_map/ppermute | solution.py:284
  76.6 38.2 %collective-permute-start.20 = (bf16[192,2048]{1,0:T(8,128)(2,1)}, bf16[192,2048]{1,0:T(8,128)(2,1)S(1)}, u32[]{:S(2)}, u32[]{:S(2)}) collective-permute-start(bf16[192,2048]{1,0:T(8,128)(2,1)} %get-tuple-element.210), channel_id=1, source_target_pairs={{0,4},{4,0},{8,12},{12,8},{1,5},{5,1},{9,13},{13,9},{2,6},{6,2},{1... | collective-permute-start | bytes 2359304 | tf_op jit(solution)/shard_map/ppermute | solution.py:284
  77.2 37.6 %collective-permute-start.19 = (bf16[128,2048]{1,0:T(8,128)(2,1)}, bf16[128,2048]{1,0:T(8,128)(2,1)S(1)}, u32[]{:S(2)}, u32[]{:S(2)}) collective-permute-start(bf16[128,2048]{1,0:T(8,128)(2,1)} %get-tuple-element.209), channel_id=1, source_target_pairs={{0,12},{4,8},{8,4},{12,0},{1,13},{5,9},{9,5},{13,1},{2,14},{6,10},... | collective-permute-start | bytes 1572872 | tf_op jit(solution)/shard_map/ppermute | solution.py:284
  79.9 34.9 %collective-permute-start.18 = (bf16[64,2048]{1,0:T(8,128)(2,1)}, bf16[64,2048]{1,0:T(8,128)(2,1)S(1)}, u32[]{:S(2)}, u32[]{:S(2)}) collective-permute-start(bf16[64,2048]{1,0:T(8,128)(2,1)} %get-tuple-element.208), channel_id=1, source_target_pairs={{0,8},{4,12},{8,0},{12,4},{1,9},{5,13},{9,1},{13,5},{2,10},{6,14},... | collective-permute-start | bytes 786440 | tf_op jit(solution)/shard_map/ppermute | solution.py:284
  80.5 15.5 %copy-start.2 = (s32[16,1]{0,1:T(1,128)S(1)}, s32[16,1]{0,1:T(1,128)}, u32[]{:S(2)}) copy-start(s32[16,1]{0,1:T(1,128)} %copy-done.1) | copy-start | bytes 196
  80.5 15.5 %copy-start.4 = (s32[16,1]{0,1:T(1,128)S(1)}, s32[16,1]{0,1:T(1,128)}, u32[]{:S(2)}) copy-start(s32[16,1]{0,1:T(1,128)} %copy-done.3) | copy-start | bytes 196
  80.5 15.5 %copy-start.6 = (s32[16,1]{0,1:T(1,128)S(1)}, s32[16,1]{0,1:T(1,128)}, u32[]{:S(2)}) copy-start(s32[16,1]{0,1:T(1,128)} %copy-done.5) | copy-start | bytes 196
  80.5 15.6 %copy-start.7 = (s32[16,1]{0,1:T(1,128)S(1)}, s32[16,1]{0,1:T(1,128)}, u32[]{:S(2)}) copy-start(s32[16,1]{0,1:T(1,128)} %param.26) | copy-start | bytes 196
  80.5 15.6 %copy-start.8 = (s32[3]{0:T(128)S(1)}, s32[3]{0:T(128)}, u32[]{:S(2)}) copy-start(s32[3]{0:T(128)} %add_xor_fusion) | copy-start | bytes 40
  116.8 31.3 %collective-permute-start.7 = (bf16[256,2048]{1,0:T(8,128)(2,1)S(1)}, bf16[256,2048]{1,0:T(8,128)(2,1)S(1)}, u32[]{:S(2)}, u32[]{:S(2)}) collective-permute-start(bf16[256,2048]{1,0:T(8,128)(2,1)S(1)} %get-tuple-element.128), channel_id=1, source_target_pairs={{0,8},{4,12},{8,0},{12,4},{1,9},{5,13},{9,1},{13,5},{2,10},{6,14},... | collective-permute-start | bytes 3145736 | tf_op jit(solution)/shard_map/cond/branch_4_fun/ppermute | solution.py:284
